TPU v7x, 32 devices: a whole 2x2x4 slice. The times are simulated.
32 devices in a mesh: groups: 2 (over y), ctx: 4 (over z), heads: 2 (over x), sub: 2 (over core).
Axes of the slice: x: 2, y: 2, z: 4, core: 2. Of those that a mesh axis runs over, the one named last changes fastest.
Arguments:
- queries: bfloat16 [2048, 4096], P(('groups', 'ctx', 'sub'), 'heads'), parts along dimension 0, may hold values from -6 to 6
- keys: bfloat16 [2048, 1024], P(('groups', 'ctx'), 'heads'), parts along dimension 0, may hold values from -6 to 6
- values: bfloat16 [2048, 1024], P(('groups', 'ctx'), 'heads'), parts along dimension 0, may hold values from -6 to 6
- image_keys: bfloat16 [256, 1024], P(('groups', 'ctx', 'sub'), 'heads'), parts along dimension 0, may hold values from -6 to 6
- image_values: bfloat16 [256, 1024], P(('groups', 'ctx', 'sub'), 'heads'), parts along dimension 0, may hold values from -6 to 6
- image_lengths: int32 [16], P('groups'), parts along dimension 0, may hold values from 1 to 32, 128 in all
- token_images: int32 [2048], P('groups'), parts along dimension 0, may hold values from 0 to 8, as said below
Outputs:
- self_out: bfloat16 [2048, 4096], P(('groups', 'ctx', 'sub'), 'heads'), parts along dimension 0
- cross_out: bfloat16 [2048, 4096], P(('groups', 'ctx', 'sub'), 'heads'), parts along dimension 0
There are 2 independent parts, one for each index of `groups`. A program takes and returns all parts, laid end to end along the dimension named above; each array names one. Nothing has to cross between parts.
Inputs may be any that keep to these rules, and one draw needn't show every extreme that they name: `token_images`: never falls along the sequence; the first token sees no image and the last sees all 8.
All inputs are finite; a program needn't handle non-finite values.
Results may differ from a plain program's by a relative error of at most 0.005.
Values may be sent and summed in bfloat16 or wider, within the bound.
A program may use at most 128 MiB of HBM per device.

v0:
```python
import math

import jax
import jax.numpy as jnp
from jax import lax
from jax.sharding import PartitionSpec as P

QH = 32
KVH = 8
HD = 128
NIMG = 8


def online(state, query_view, key_block, value_block, allowed):
    run_max, run_sum, run_out = state
    scores = jnp.einsum(
        "rhgd,khd->hgrk", query_view, key_block, preferred_element_type=jnp.float32
    ) * (1.0 / math.sqrt(HD))
    scores = jnp.where(allowed[None, None], scores, -1e30)
    new_max = jnp.maximum(run_max, jnp.max(scores, axis=-1))
    weights = jnp.exp(scores - new_max[..., None])
    factor = jnp.exp(run_max - new_max)
    run_sum = run_sum * factor + jnp.sum(weights, axis=-1)
    run_out = run_out * factor[..., None] + jnp.einsum(
        "hgrk,khd->hgrd",
        weights.astype(jnp.bfloat16),
        value_block,
        preferred_element_type=jnp.float32,
    )
    return (new_max, run_sum, run_out)


def local(queries, keys, values, image_keys, image_values, image_lengths, token_images):
    cycle_pos = lax.axis_index("ctx")
    core_pos = lax.axis_index("sub")
    core_count = lax.axis_size("sub")
    tok_rows = queries.shape[0]
    group_size = QH // KVH
    offset = core_pos * tok_rows
    text_k, text_v = (keys, values)
    ctx_span = core_count * tok_rows
    first_row = cycle_pos * ctx_span + offset
    positions = first_row + jnp.arange(tok_rows, dtype=jnp.int32)
    images_seen = lax.dynamic_slice_in_dim(token_images, first_row, tok_rows)
    image_index = jnp.arange(NIMG, dtype=jnp.int32)
    visible = jnp.sum(
        jnp.where(image_index[None, :] < images_seen[:, None], image_lengths[None, :], 0), axis=1
    )
    heads_here = text_k.shape[1] // HD
    query_view = queries.reshape(tok_rows, heads_here, group_size, HD)
    start_state = (
        jnp.full((heads_here, group_size, tok_rows), -1e29, jnp.float32),
        jnp.zeros((heads_here, group_size, tok_rows), jnp.float32),
        jnp.zeros((heads_here, group_size, tok_rows, HD), jnp.float32),
    )
    last_position = jnp.max(positions)
    most_visible = jnp.max(visible)
    key_block = lax.all_gather(text_k, "ctx", axis=0, tiled=True).reshape(-1, heads_here, HD)
    value_block = lax.all_gather(text_v, "ctx", axis=0, tiled=True).reshape(-1, heads_here, HD)
    key_pos = jnp.arange(key_block.shape[0], dtype=jnp.int32)
    allowed = key_pos[None, :] <= positions[:, None]
    self_state = lax.cond(
        jnp.int32(0) > last_position,
        lambda inner: inner,
        lambda inner: online(inner, query_view, key_block, value_block, allowed),
        start_state,
    )
    gathered_k, gathered_v = (
        lax.all_gather(image_keys, ("ctx", "sub"), axis=0, tiled=True),
        lax.all_gather(image_values, ("ctx", "sub"), axis=0, tiled=True),
    )
    image_rows = gathered_k.shape[0]
    block_rows = min(256, image_rows)
    block_count = image_rows // block_rows
    blocks_k = gathered_k.reshape(block_count, block_rows, heads_here, HD)
    blocks_v = gathered_v.reshape(block_count, block_rows, heads_here, HD)
    block_firsts = jnp.arange(block_count, dtype=jnp.int32) * block_rows

    def cross_step(state, inputs):
        key_block, value_block, first = inputs
        key_pos = first + jnp.arange(block_rows, dtype=jnp.int32)
        allowed = key_pos[None, :] < visible[:, None]
        updated = lax.cond(
            first >= most_visible,
            lambda inner: inner,
            lambda inner: online(inner, query_view, key_block, value_block, allowed),
            state,
        )
        return (updated, None)

    cross_state, _ = lax.scan(cross_step, start_state, (blocks_k, blocks_v, block_firsts))
    self_result = self_state[2] / self_state[1][..., None]
    has_image = visible > 0
    safe_sum = jnp.where(has_image[None, None, :], cross_state[1], 1.0)
    cross_result = jnp.where(
        has_image[None, None, :, None], cross_state[2] / safe_sum[..., None], 0.0
    )
    self_out = (
        self_result.transpose(2, 0, 1, 3)
        .reshape(tok_rows, heads_here * group_size * HD)
        .astype(jnp.bfloat16)
    )
    cross_out = (
        cross_result.transpose(2, 0, 1, 3)
        .reshape(tok_rows, heads_here * group_size * HD)
        .astype(jnp.bfloat16)
    )
    return (self_out, cross_out)


def solution(mesh):
    in_specs = (
        P(("groups", "ctx", "sub"), "heads"),
        P(("groups", "ctx"), "heads"),
        P(("groups", "ctx"), "heads"),
        P(("groups", "ctx", "sub"), "heads"),
        P(("groups", "ctx", "sub"), "heads"),
        P("groups"),
        P("groups"),
    )
    out_specs = (P(("groups", "ctx", "sub"), "heads"), P(("groups", "ctx", "sub"), "heads"))
    return jax.shard_map(local, mesh=mesh, in_specs=in_specs, out_specs=out_specs, check_vma=False)
```

profile of v0, /device:TPU:0, one launch (start us, length us, event | category | flops | bytes accessed | tf_op | source)
XLA Modules:
  0.0 92.7 jit_solution(3019810822023664031)
XLA Ops:
  7.2 0.0 all-gather.3.cloned.1.call-start
  7.2 0.7 all-gather.3.cloned.1.call-update
  7.9 0.0 all-gather.5.cloned.1.call-start
  7.9 0.7 all-gather.5.cloned.1.call-update
  8.7 0.6 add_reduce_fusion
  9.9 1.3 %copy.34 = bf16[128,2048]{0,1:T(8,128)(2,1)S(1)} copy(bf16[128,2048]{1,0:T(8,128)(2,1)} %param.11) | data formatting | bytes 1048576 | tf_op args[0]
  11.3 0.8 dynamic_slice.11
  12.0 0.7 select_reduce_fusion
  12.8 0.6 reduce_max.39
  14.1 0.1 broadcast_in_dim.109
  14.2 16.3 %all_gather.14 = bf16[128,512]{1,0:T(8,128)(2,1)S(1)} all-gather(bf16[16,512]{1,0:T(8,128)(2,1)} %param.14), channel_id=1, replica_groups=mesh['groups'=2,'ctx'=4,'heads'=2,'sub'=2] {'ctx','sub'}, dimensions={0}, use_global_device_ids=true | all-gather | bytes 147456 | tf_op jit(solution)/shard_map/all_gather | solution.py:69
  30.4 14.5 %all_gather.15 = bf16[128,512]{1,0:T(8,128)(2,1)S(1)} all-gather(bf16[16,512]{1,0:T(8,128)(2,1)} %param.15), channel_id=1, replica_groups=mesh['groups'=2,'ctx'=4,'heads'=2,'sub'=2] {'ctx','sub'}, dimensions={0}, use_global_device_ids=true | all-gather | bytes 147456 | tf_op jit(solution)/shard_map/all_gather | solution.py:70
  45.0 1.4 %conditional.3 = ((f32[4,4,128]{2,1,0:T(4,128)S(1)}, f32[4,4,128,128]{3,2,1,0:T(8,128)S(1)})) conditional(s32[]{:T(128)} %convert_element_type.37, (s32[1,128]{1,0:T(1,128)S(1)}, s32[128]{0:T(128)S(1)}, bf16[128,512]{1,0:T(8,128)(2,1)S(1)}, bf16[128,4,4,128]{0,3,2,1:T(8,128)(2,1)S(1)}, f32[4,4,128]{2,1,0:T(4,128)S(1)}, ...), branch_computations={%region_7.10_spmd, %region_10.11_spmd} | conditional | flops 136599552 | bytes 6685720 | solution.py:83
  45.0 0.1 broadcast_compare_fusion.1
  45.1 0.3 fusion.25
  45.4 0.2 fusion.18
  45.6 0.7 convolution_add_fusion
  46.4 0.4 fusion.24
  46.7 0.4 copy.38
  47.1 1.2 %convert_element_type.40 = bf16[128,2048]{1,0:T(8,128)(2,1)} reshape(bf16[128,4,4,128]{3,2,1,0:T(4,128)(2,1)S(1)} %copy.38) | data formatting | bytes 1048576 | tf_op jit(solution)/shard_map/convert_element_type | solution.py:106
  48.3 22.5 %all-gather.5.cloned.1.call-done = bf16[1024,512]{1,0:T(8,128)(2,1)} async-done(((bf16[256,512]{1,0:T(8,128)(2,1)}), bf16[1024,512]{1,0:T(8,128)(2,1)}) %all-gather.5.cloned.1.call-update) | async-done | bytes 1048592 | tf_op jit(solution)/shard_map/all_gather | solution.py:59
  70.9 13.1 %conditional.2 = (f32[4,4,128]{2,1,0:T(4,128)S(1)}, f32[4,4,128,128]{3,2,1,0:T(8,128)S(1)}) conditional(s32[]{:T(128)} %convert_element_type.33, (s32[]{:T(128)}, s32[128,1]{0,1:T(1,128)S(1)}, s32[128,1024]{0,1:T(8,128)S(1)}, bf16[1024,512]{1,0:T(8,128)(2,1)}, bf16[128,4,4,128]{0,3,2,1:T(8,128)(2,1)S(1)}, ...), branch_computations={%region_1.4_spmd, %region_4.5_spmd} | conditional | flops 1097209984 | bytes 71919184 | solution.py:62
  70.9 0.1 broadcast_compare_fusion
  71.0 1.3 %reshape.44 = bf16[1024,4,128]{2,1,0:T(4,128)(2,1)S(1)} reshape(bf16[1024,512]{1,0:T(8,128)(2,1)} %get-tuple-element.110) | data formatting | bytes 2097152 | tf_op jit(solution)/shard_map/reshape | solution.py:58
  72.3 1.4 %fusion.2 = (f32[4,4,128]{2,1,0:T(4,128)S(1)}, f32[4,1024,128,4]{2,1,3,0:T(8,128)S(1)}) fusion(pred[128,1024]{0,1:T(8,128)(4,1)S(1)} %broadcast_compare_fusion, bf16[128,4,4,128]{0,3,2,1:T(8,128)(2,1)S(1)} %get-tuple-element.147, bf16[1024,4,128,1]{2,1,0,3:T(4,128)(2,1)S(1)} %bitcast.31), kind=kOutput, calls=%fused_computation.4 | convolution fusion | flops 543160320 | bytes 10100736 | tf_op jit(solution)/shard_map/cond/branch_0_fun/rhgd,khd->hgrk/dot_general | solution.py:16
  73.7 3.2 %copy-done = f32[4,1024,128,4]{2,1,3,0:T(8,128)} copy-done((f32[4,1024,128,4]{2,1,3,0:T(8,128)}, f32[4,1024,128,4]{2,1,3,0:T(8,128)S(1)}, u32[]{:S(2)}) %copy-start) | copy-done | bytes 8388632 | tf_op jit(solution)/shard_map/cond
  76.9 1.8 %fusion.1 = f32[4,4,128]{2,1,0:T(4,128)S(1)} fusion(f32[4,1024,128,4]{2,1,3,0:T(8,128)S(1)} %get-tuple-element.159, f32[4,4,128]{2,1,0:T(4,128)S(1)} %broadcast_maximum_fusion, pred[128,1024]{0,1:T(8,128)(4,1)S(1)} %broadcast_compare_fusion), kind=kLoop, calls=%fused_computation.3 | loop fusion | flops 8386560 | bytes 8536064 | tf_op jit(solution)/shard_map/cond/branch_0_fun/reduce_sum | solution.py:23
  78.7 0.3 reshape.45
  79.0 4.9 %fusion.6 = f32[4,4,128,128]{3,2,1,0:T(8,128)S(1)} fusion(f32[4,1024,128,4]{2,1,3,0:T(8,128)} %copy-done, f32[4,4,128]{2,1,0:T(4,128)S(1)} %broadcast_maximum_fusion, pred[128,1024]{0,1:T(8,128)(4,1)S(1)} %broadcast_compare_fusion, bf16[1024,4,128,1]{2,1,0,3:T(4,128)(2,1)S(1)} %bitcast.32, f32[4,4,128]{2,1,0:T(4,128)S(1)} %get-tuple-element.156), kind=kOutput, calls=%fused_computation.7 | convolution fusion | flops 545521664 | bytes 10633216 | tf_op jit(solution)/shard_map/cond/branch_0_fun/hgrk,khd->hgrd/dot_general | solution.py:24
  83.9 0.3 fusion.23
  84.3 0.4 copy.36
  84.7 1.2 %convert_element_type.36 = bf16[128,2048]{1,0:T(8,128)(2,1)} reshape(bf16[128,4,4,128]{3,2,1,0:T(4,128)(2,1)S(1)} %copy.36) | data formatting | bytes 1048576 | tf_op jit(solution)/shard_map/convert_element_type | solution.py:101
  (17 shorter events, 0.2 us)
Async XLA Ops:
  7.2 41.2 %all-gather.3.cloned.1.call-start = ((), (), s32[]{:S(2)}) async-start(), calls=%async_computation | async-start | bytes 1310720 | tf_op jit(solution)/shard_map/all_gather | solution.py:58
  7.9 62.9 %all-gather.5.cloned.1.call-start = ((), (), s32[]{:S(2)}) async-start(), calls=%async_computation.1 | async-start | bytes 1310720 | tf_op jit(solution)/shard_map/all_gather | solution.py:59
  72.3 6.4 %copy-start.1 = (bf16[1024,512]{1,0:T(8,128)(2,1)S(1)}, bf16[1024,512]{1,0:T(8,128)(2,1)}, u32[]{:S(2)}) copy-start(bf16[1024,512]{1,0:T(8,128)(2,1)} %get-tuple-element.112) | copy-start | bytes 3145732 | tf_op jit(solution)/shard_map/cond
  73.7 3.2 %copy-start = (f32[4,1024,128,4]{2,1,3,0:T(8,128)}, f32[4,1024,128,4]{2,1,3,0:T(8,128)S(1)}, u32[]{:S(2)}) copy-start(f32[4,1024,128,4]{2,1,3,0:T(8,128)S(1)} %get-tuple-element.159) | copy-start | bytes 25165828 | tf_op jit(solution)/shard_map/cond
Sparse Core Ops, SparseCore 0:
  9.6 31.8 all-gather.2
  43.0 27.7 all-gather.4
where the time goes:
time: 93 us; the launch traced here: 92.7 us
  blocking collectives  30.8 us (33%)
  waiting for transfers between devices  23.9 us (26%)
  between operations  15.4 us (17%)
  local copies, waits for them, and re-layouts  10.3 us (11%)
  matrix products  7.26 us (8%)
  other arithmetic  4.85 us (5%)
    all_gather x1, waiting for transfers between devices, local(): lax.all_gather(text_v, 'ctx', axis=0, tiled=True)  22.5 us
    all_gather x1, blocking collectives, local(): lax.all_gather(image_keys, ('ctx', 'sub'), axis=0, tiled=True)  16.3 us
    all_gather x1, blocking collectives, local(): lax.all_gather(image_values, ('ctx', 'sub'), axis=0, tiled=True)  14.5 us
    dot_general x2, matrix products, online(): jnp.einsum('hgrk,khd->hgrd', weights.astype(jnp.bfloat16), value_block, p...  5.59 us
    cond x4, local copies, waits for them, and re-layouts  3.21 us
    reduce_sum x2, other arithmetic, online(): run_sum = run_sum * factor + jnp.sum(weights, axis=-1)  1.92 us
  transfers between devices with their start and end apart: 2, of which 1 were waited for; matrix products, arithmetic and copies ran while one was open for 8% of the time, Pallas kernels for 0%

commit v1 on v0

v1 whole, which is shorter than its diff:
```python
import functools
import math

import jax
import jax.numpy as jnp
from jax import lax
from jax.experimental import pallas as pl
from jax.experimental.pallas import tpu as pltpu
from jax.sharding import PartitionSpec as P

HD = 128
MESH = pl.DeviceIdType.MESH
LOW = -1e30
SCALE = math.log2(math.e) / math.sqrt(HD)


def kernel(
    n, subs, lengths, tokens, q_hbm, k_hbm, v_hbm, ik_hbm, iv_hbm, self_ref, cross_ref,
    q, k, v, qt, kv, img, run_max, run_sum, run_out,
    in_sem, text_recv, up_send, side_send, img_recv, img_send, img_side,
):
    c, s = lax.axis_index("ctx"), lax.axis_index("sub")
    rows, span = q.shape[0], k.shape[0]
    heads = k.shape[1] // HD
    share = heads // subs
    group = q.shape[1] // k.shape[1]
    image_rows = img.shape[2]
    mine = c * subs + s

    def sibling(d):
        return {"sub": lax.rem(s + d, subs)}

    loads = [
        pltpu.make_async_copy(src, dst, in_sem.at[i])
        for i, (src, dst) in enumerate(
            [(k_hbm, k), (v_hbm, v), (ik_hbm, img.at[mine, 0]), (iv_hbm, img.at[mine, 1]), (q_hbm, q)]
        )
    ]
    for load in loads:
        load.start()

    barrier = pltpu.get_barrier_semaphore()

    @pl.loop(1, n)
    def _(d):
        pl.semaphore_signal(barrier, inc=1, device_id={"ctx": lax.rem(c + d, n)}, device_id_type=MESH)

    for d in range(1, subs):
        pl.semaphore_signal(barrier, inc=1, device_id=sibling(d), device_id_type=MESH)

    loads[0].wait()
    for j in range(heads):
        kv[c, j, 0] = k[:, j * HD:(j + 1) * HD]
    loads[1].wait()
    for j in range(heads):
        for i in range(span // HD):
            kv[c, j, 1, i * HD:(i + 1) * HD] = v[i * HD:(i + 1) * HD, j * HD:(j + 1) * HD].T
    loads[2].wait()
    loads[3].wait()
    pl.semaphore_wait(barrier, n - 1 + subs - 1)

    def up(b, i):
        j = s * share + i
        return pltpu.make_async_remote_copy(
            kv.at[b, j], kv.at[b, j], up_send.at[b, i], text_recv.at[b, j],
            device_id={"ctx": lax.rem(c + 1, n)}, device_id_type=MESH,
        )

    def side(b, j, i, d):
        return pltpu.make_async_remote_copy(
            kv.at[b, j], kv.at[b, j], side_send.at[b, i, d - 1], text_recv.at[b, j],
            device_id=sibling(d), device_id_type=MESH,
        )

    def image_to(d):
        return pltpu.make_async_remote_copy(
            img.at[mine], img.at[mine], img_send.at[d - 1], img_recv.at[mine],
            device_id={"ctx": lax.rem(c + d, n)}, device_id_type=MESH,
        )

    def image_side(cc, ss, d):
        at = cc * subs + ss
        return pltpu.make_async_remote_copy(
            img.at[at], img.at[at], img_side.at[cc, d - 1], img_recv.at[at],
            device_id=sibling(d), device_id_type=MESH,
        )

    @pl.loop(1, n)
    def _(d):
        image_to(d).start()

    for d in range(1, subs):
        image_side(c, s, d).start()

    @pl.when(c < n - 1)
    def _():
        for i in range(share):
            up(c, i).start()

    loads[4].wait()
    for j in range(heads):
        for g in range(group):
            h = j * group + g
            qt[j, :, g * rows:(g + 1) * rows] = q[:, h * HD:(h + 1) * HD].T

    def scores(j, key_rows):
        return jnp.dot(key_rows, qt[j], preferred_element_type=jnp.float32) * SCALE

    def wide(x):
        return jnp.concatenate([x] * group, axis=1)

    def put(ref, j, out):
        out = out.astype(jnp.bfloat16)
        for g in range(group):
            at = pl.multiple_of((j * group + g) * HD, HD)
            ref[:, pl.ds(at, HD)] = out[:, g * rows:(g + 1) * rows].T

    def values_of(b, j):
        return jnp.concatenate([kv[b, j, 1, i * HD:(i + 1) * HD] for i in range(span // HD)], axis=1)

    def finish(j):
        put(self_ref, j, run_out[j] * (1.0 / run_sum[j]))

    key_at = lax.broadcasted_iota(jnp.int32, (span, rows), 0)
    row_at = lax.broadcasted_iota(jnp.int32, (span, rows), 1) + s * rows
    bias = wide(jnp.where(key_at <= row_at, 0.0, LOW))
    for j in range(heads):
        sc = scores(j, kv[c, j, 0]) + bias
        top = jnp.max(sc, axis=0, keepdims=True)
        w = jnp.exp2(sc - top)
        run_max[j] = top
        run_sum[j] = jnp.sum(w, axis=0, keepdims=True)
        run_out[j] = jnp.dot(values_of(c, j), w.astype(jnp.bfloat16), preferred_element_type=jnp.float32)

    @pl.when(c == 0)
    def _():
        for j in range(heads):
            finish(j)

    @pl.loop(1, n)
    def _(d):
        cc = lax.rem(c + d, n)
        image_side(cc, s, 1).wait_recv()
        for e in range(1, subs):
            image_side(cc, s, e).start()

    @pl.loop(0, n)
    def _(cc):
        for e in range(1, subs):
            image_side(cc, lax.rem(s + e, subs), e).wait_recv()

    seen_images = tokens[pl.ds(mine, 1), :]
    visible = jnp.zeros_like(seen_images)
    for i in range(lengths.shape[0]):
        visible = visible + jnp.where(seen_images > i, lengths[i], 0)
    visible = wide(visible)
    count = n * subs * image_rows
    allowed = lax.broadcasted_iota(jnp.int32, (count, group * rows), 0) < visible
    for j in range(heads):
        cols = slice(j * HD, (j + 1) * HD)
        sc = jnp.where(allowed, scores(j, img[:, 0, :, cols].reshape(count, HD)), LOW)
        top = jnp.max(sc, axis=0, keepdims=True)
        w = jnp.where(allowed, jnp.exp2(sc - top), 0.0)
        total = jnp.sum(w, axis=0, keepdims=True)
        out = jnp.dot(
            img[:, 1, :, cols].reshape(count, HD).T, w.astype(jnp.bfloat16),
            preferred_element_type=jnp.float32,
        )
        out = jnp.where(visible > 0, out * (1.0 / jnp.where(visible > 0, total, 1.0)), 0.0)
        put(cross_ref, j, out)

    def attend(b, j):
        sc = scores(j, kv[b, j, 0])
        old = run_max[j]
        top = jnp.maximum(old, jnp.max(sc, axis=0, keepdims=True))
        w = jnp.exp2(sc - top)
        factor = jnp.exp2(old - top)
        run_max[j] = top
        run_sum[j] = run_sum[j] * factor + jnp.sum(w, axis=0, keepdims=True)
        run_out[j] = run_out[j] * factor + jnp.dot(
            values_of(b, j), w.astype(jnp.bfloat16), preferred_element_type=jnp.float32
        )

        @pl.when(b == 0)
        def _():
            finish(j)

    @pl.loop(1, c + 1)
    def _(t):
        b = c - t
        for i in range(share):
            up(b, i).wait_recv()

            @pl.when(c < n - 1)
            def _():
                up(b, i).start()

            for d in range(1, subs):
                side(b, s * share + i, i, d).start()
            attend(b, s * share + i)
            for d in range(1, subs):
                j = lax.rem(s + d, subs) * share + i
                side(b, j, i, d).wait_recv()
                attend(b, j)

    @pl.loop(1, n)
    def _(d):
        image_to(d).wait_send()

    @pl.loop(0, n)
    def _(cc):
        for d in range(1, subs):
            image_side(cc, s, d).wait_send()

    @pl.when(c < n - 1)
    def _():
        @pl.loop(0, c + 1)
        def _(b):
            for i in range(share):
                up(b, i).wait_send()

    @pl.loop(0, c)
    def _(b):
        for i in range(share):
            for d in range(1, subs):
                side(b, s * share + i, i, d).wait_send()


def local(queries, keys, values, image_keys, image_values, image_lengths, token_images):
    n, subs = lax.axis_size("ctx"), lax.axis_size("sub")
    rows, wide = queries.shape
    span, narrow = keys.shape
    heads, image_rows = narrow // HD, image_keys.shape[0]
    group = wide // narrow
    share = heads // subs
    vmem = pl.BlockSpec(memory_space=pltpu.VMEM)
    hbm = pl.BlockSpec(memory_space=pl.ANY)
    dma = pltpu.SemaphoreType.DMA
    out = jax.ShapeDtypeStruct((rows, wide), jnp.bfloat16)
    return pl.pallas_call(
        functools.partial(kernel, n, subs),
        out_shape=(out, out),
        in_specs=[pl.BlockSpec(memory_space=pltpu.SMEM), vmem, hbm, hbm, hbm, hbm, hbm],
        out_specs=(vmem, vmem),
        scratch_shapes=[
            pltpu.VMEM((rows, wide), jnp.bfloat16),
            pltpu.VMEM((span, narrow), jnp.bfloat16),
            pltpu.VMEM((span, narrow), jnp.bfloat16),
            pltpu.VMEM((heads, HD, group * rows), jnp.bfloat16),
            pltpu.VMEM((n, heads, 2, span, HD), jnp.bfloat16),
            pltpu.VMEM((n * subs, 2, image_rows, narrow), jnp.bfloat16),
            pltpu.VMEM((heads, 1, group * rows), jnp.float32),
            pltpu.VMEM((heads, 1, group * rows), jnp.float32),
            pltpu.VMEM((heads, HD, group * rows), jnp.float32),
            dma((5,)),
            dma((n, heads)),
            dma((n, share)),
            dma((n, share, subs - 1)),
            dma((n * subs,)),
            dma((n - 1,)),
            dma((n, subs - 1)),
        ],
        compiler_params=pltpu.CompilerParams(
            collective_id=0, has_side_effects=True, vmem_limit_bytes=40 * 1024 * 1024
        ),
    )(image_lengths, token_images.reshape(-1, rows), queries, keys, values, image_keys, image_values)


def solution(mesh):
    fine = P(("groups", "ctx", "sub"), "heads")
    block = P(("groups", "ctx"), "heads")
    in_specs = (fine, block, block, fine, fine, P("groups"), P("groups"))
    return jax.shard_map(local, mesh=mesh, in_specs=in_specs, out_specs=(fine, fine), check_vma=False)
```

time: 93 us -> 33.7 us (0.36)
  the two profiles are of different devices: /device:TPU:0 before, /device:TPU:29 now
where the time goes in v1:
time: 33.7 us; the launch traced here: 33.3 us
  Pallas kernels  25.3 us (75%)
  local copies, waits for them, and re-layouts  7.3 us (22%)
  between operations  0.66 us (2%)
    pallas_call x1, Pallas kernels, local(): pl.pallas_call(functools.partial(kernel, n, subs), out_shape=(out, out),...  25.3 us
    unnamed x16, local copies, waits for them, and re-layouts  7.3 us

profile of v1, /device:TPU:29, one launch (start us, length us, event | category | flops | bytes accessed | tf_op | source)
XLA Modules:
  0.0 33.3 jit_solution(726053880079983322)
XLA Ops:
  0.6 0.0 copy-start.6
  0.6 0.6 %copy-done.6 = s32[8]{0:T(128)S(1)} copy-done((s32[8]{0:T(128)S(1)}, s32[8]{0:T(128)}, u32[]{:S(2)}) %copy-start.6) | copy-done | bytes 56
  1.3 0.0 copy-start
  1.3 1.0 %copy-done = bf16[128,2048]{1,0:T(8,128)(2,1)S(1)} copy-done((bf16[128,2048]{1,0:T(8,128)(2,1)S(1)}, bf16[128,2048]{1,0:T(8,128)(2,1)}, u32[]{:S(2)}) %copy-start) | copy-done | bytes 524312
  2.3 0.0 copy-start.1
  2.3 0.9 %copy-done.1 = bf16[256,512]{1,0:T(8,128)(2,1)S(1)} copy-done((bf16[256,512]{1,0:T(8,128)(2,1)S(1)}, bf16[256,512]{1,0:T(8,128)(2,1)}, u32[]{:S(2)}) %copy-start.1) | copy-done | bytes 262168
  3.3 0.0 copy-start.2
  3.3 0.9 %copy-done.2 = bf16[256,512]{1,0:T(8,128)(2,1)S(1)} copy-done((bf16[256,512]{1,0:T(8,128)(2,1)S(1)}, bf16[256,512]{1,0:T(8,128)(2,1)}, u32[]{:S(2)}) %copy-start.2) | copy-done | bytes 262168
  4.2 0.0 copy-start.3
  4.2 0.7 %copy-done.3 = bf16[16,512]{1,0:T(8,128)(2,1)S(1)} copy-done((bf16[16,512]{1,0:T(8,128)(2,1)S(1)}, bf16[16,512]{1,0:T(8,128)(2,1)}, u32[]{:S(2)}) %copy-start.3) | copy-done | bytes 16408
  4.9 0.0 copy-start.4
  5.0 0.7 %copy-done.4 = bf16[16,512]{1,0:T(8,128)(2,1)S(1)} copy-done((bf16[16,512]{1,0:T(8,128)(2,1)S(1)}, bf16[16,512]{1,0:T(8,128)(2,1)}, u32[]{:S(2)}) %copy-start.4) | copy-done | bytes 16408
  5.7 0.0 copy-start.5
  5.7 0.7 %copy-done.5 = s32[1024]{0:T(1024)S(1)} copy-done((s32[1024]{0:T(1024)S(1)}, s32[1024]{0:T(1024)}, u32[]{:S(2)}) %copy-start.5) | copy-done | bytes 4120
  6.4 25.3 %shard_map.86 = (bf16[128,2048]{1,0:T(8,128)(2,1)S(1)}, bf16[128,2048]{1,0:T(8,128)(2,1)S(1)}) custom-call(s32[8]{0:T(128)S(1)} %copy-done.6, s32[8,128]{1,0:T(8,128)S(1)} %bitcast.1, bf16[128,2048]{1,0:T(8,128)(2,1)S(1)} %copy-done, bf16[256,512]{1,0:T(8,128)(2,1)S(1)} %copy-done.1, bf16[256,512]{1,0:T(8,128)(2,1)S(1)} %copy-done.2, ...), custom_call_target="tpu_custom_call" | custom-call | tf_op jit(solution)/shard_map/pallas_call | solution.py:240
  31.7 0.8 %copy.11 = bf16[128,2048]{1,0:T(8,128)(2,1)} copy(bf16[128,2048]{1,0:T(8,128)(2,1)S(1)} %get-tuple-element.4) | data formatting | bytes 1048576
  32.5 0.8 %copy.12 = bf16[128,2048]{1,0:T(8,128)(2,1)} copy(bf16[128,2048]{1,0:T(8,128)(2,1)S(1)} %get-tuple-element.5) | data formatting | bytes 1048576
Async XLA Ops:
  0.6 0.7 %copy-start.6 = (s32[8]{0:T(128)S(1)}, s32[8]{0:T(128)}, u32[]{:S(2)}) copy-start(s32[8]{0:T(128)} %lengths.1) | copy-start | bytes 100
  1.3 1.0 %copy-start = (bf16[128,2048]{1,0:T(8,128)(2,1)S(1)}, bf16[128,2048]{1,0:T(8,128)(2,1)}, u32[]{:S(2)}) copy-start(bf16[128,2048]{1,0:T(8,128)(2,1)} %q_hbm.1) | copy-start | bytes 1572868
  2.3 0.9 %copy-start.1 = (bf16[256,512]{1,0:T(8,128)(2,1)S(1)}, bf16[256,512]{1,0:T(8,128)(2,1)}, u32[]{:S(2)}) copy-start(bf16[256,512]{1,0:T(8,128)(2,1)} %k_hbm.1) | copy-start | bytes 786436
  3.3 0.9 %copy-start.2 = (bf16[256,512]{1,0:T(8,128)(2,1)S(1)}, bf16[256,512]{1,0:T(8,128)(2,1)}, u32[]{:S(2)}) copy-start(bf16[256,512]{1,0:T(8,128)(2,1)} %v_hbm.1) | copy-start | bytes 786436
  4.2 0.7 %copy-start.3 = (bf16[16,512]{1,0:T(8,128)(2,1)S(1)}, bf16[16,512]{1,0:T(8,128)(2,1)}, u32[]{:S(2)}) copy-start(bf16[16,512]{1,0:T(8,128)(2,1)} %ik_hbm.1) | copy-start | bytes 49156
  4.9 0.7 %copy-start.4 = (bf16[16,512]{1,0:T(8,128)(2,1)S(1)}, bf16[16,512]{1,0:T(8,128)(2,1)}, u32[]{:S(2)}) copy-start(bf16[16,512]{1,0:T(8,128)(2,1)} %iv_hbm.1) | copy-start | bytes 49156
  5.7 0.7 %copy-start.5 = (s32[1024]{0:T(1024)S(1)}, s32[1024]{0:T(1024)}, u32[]{:S(2)}) copy-start(s32[1024]{0:T(1024)} %param.13) | copy-start | bytes 12292

commit v2 on v1

--- a/solution.py
+++ b/solution.py
@@ -15,14 +15,14 @@
 
 
 def kernel(
-    n, subs, lengths, tokens, q_hbm, k_hbm, v_hbm, ik_hbm, iv_hbm, self_ref, cross_ref,
-    q, k, v, qt, kv, img, run_max, run_sum, run_out,
+    n, subs, len_hbm, tok_hbm, q_hbm, k_hbm, v_hbm, ik_hbm, iv_hbm, self_ref, cross_ref,
+    lengths, tokens, q, k, v, qt, kv, img, run_max, run_sum, run_out,
     in_sem, text_recv, up_send, side_send, img_recv, img_send, img_side,
 ):
     c, s = lax.axis_index("ctx"), lax.axis_index("sub")
     rows, span = q.shape[0], k.shape[0]
     heads = k.shape[1] // HD
-    share = heads // subs
+    part = span // subs
     group = q.shape[1] // k.shape[1]
     image_rows = img.shape[2]
     mine = c * subs + s
@@ -30,45 +30,50 @@
     def sibling(d):
         return {"sub": lax.rem(s + d, subs)}
 
+    barrier = pltpu.get_barrier_semaphore()
+
+    @pl.loop(1, n)
+    def _(d):
+        pl.semaphore_signal(barrier, inc=1, device_id={"ctx": lax.rem(c + d, n)}, device_id_type=MESH)
+
+    for d in range(1, subs):
+        pl.semaphore_signal(barrier, inc=1, device_id=sibling(d), device_id_type=MESH)
+
     loads = [
         pltpu.make_async_copy(src, dst, in_sem.at[i])
         for i, (src, dst) in enumerate(
-            [(k_hbm, k), (v_hbm, v), (ik_hbm, img.at[mine, 0]), (iv_hbm, img.at[mine, 1]), (q_hbm, q)]
+            [
+                (k_hbm, k), (v_hbm, v), (ik_hbm, img.at[mine, 0]), (iv_hbm, img.at[mine, 1]),
+                (q_hbm, q), (len_hbm, lengths), (tok_hbm, tokens),
+            ]
         )
     ]
     for load in loads:
         load.start()
 
-    barrier = pltpu.get_barrier_semaphore()
-
-    @pl.loop(1, n)
-    def _(d):
-        pl.semaphore_signal(barrier, inc=1, device_id={"ctx": lax.rem(c + d, n)}, device_id_type=MESH)
-
-    for d in range(1, subs):
-        pl.semaphore_signal(barrier, inc=1, device_id=sibling(d), device_id_type=MESH)
+    def lay_out(ss):
+        for j in range(heads):
+            cols = slice(j * HD, (j + 1) * HD)
+            kv[c, j, ss, 0] = k[pl.ds(ss * part, part), cols]
+            for i in range(0, part, HD):
+                kv[c, j, ss, 1, i:i + HD] = v[pl.ds(ss * part + i, HD), cols].T
 
     loads[0].wait()
-    for j in range(heads):
-        kv[c, j, 0] = k[:, j * HD:(j + 1) * HD]
     loads[1].wait()
-    for j in range(heads):
-        for i in range(span // HD):
-            kv[c, j, 1, i * HD:(i + 1) * HD] = v[i * HD:(i + 1) * HD, j * HD:(j + 1) * HD].T
+    lay_out(s)
     loads[2].wait()
     loads[3].wait()
     pl.semaphore_wait(barrier, n - 1 + subs - 1)
 
-    def up(b, i):
-        j = s * share + i
-        return pltpu.make_async_remote_copy(
-            kv.at[b, j], kv.at[b, j], up_send.at[b, i], text_recv.at[b, j],
+    def up(b, j):
+        return pltpu.make_async_remote_copy(
+            kv.at[b, j, s], kv.at[b, j, s], up_send.at[b, j], text_recv.at[b, j, s],
             device_id={"ctx": lax.rem(c + 1, n)}, device_id_type=MESH,
         )
 
-    def side(b, j, i, d):
-        return pltpu.make_async_remote_copy(
-            kv.at[b, j], kv.at[b, j], side_send.at[b, i, d - 1], text_recv.at[b, j],
+    def side(b, j, ss, d):
+        return pltpu.make_async_remote_copy(
+            kv.at[b, j, ss], kv.at[b, j, ss], side_send.at[b, j, d - 1], text_recv.at[b, j, ss],
             device_id=sibling(d), device_id_type=MESH,
         )
 
@@ -94,9 +99,11 @@
 
     @pl.when(c < n - 1)
     def _():
-        for i in range(share):
-            up(c, i).start()
-
+        for j in range(heads):
+            up(c, j).start()
+
+    for d in range(1, subs):
+        lay_out(lax.rem(s + d, subs))
     loads[4].wait()
     for j in range(heads):
         for g in range(group):
@@ -112,11 +119,18 @@
     def put(ref, j, out):
         out = out.astype(jnp.bfloat16)
         for g in range(group):
-            at = pl.multiple_of((j * group + g) * HD, HD)
+            at = (j * group + g) * HD
+            if not isinstance(at, int):
+                at = pl.multiple_of(at, HD)
             ref[:, pl.ds(at, HD)] = out[:, g * rows:(g + 1) * rows].T
 
+    def keys_of(b, j):
+        return jnp.concatenate([kv[b, j, ss, 0] for ss in range(subs)], axis=0)
+
     def values_of(b, j):
-        return jnp.concatenate([kv[b, j, 1, i * HD:(i + 1) * HD] for i in range(span // HD)], axis=1)
+        return jnp.concatenate(
+            [kv[b, j, ss, 1, i:i + HD] for ss in range(subs) for i in range(0, part, HD)], axis=1
+        )
 
     def finish(j):
         put(self_ref, j, run_out[j] * (1.0 / run_sum[j]))
@@ -125,7 +139,7 @@
     row_at = lax.broadcasted_iota(jnp.int32, (span, rows), 1) + s * rows
     bias = wide(jnp.where(key_at <= row_at, 0.0, LOW))
     for j in range(heads):
-        sc = scores(j, kv[c, j, 0]) + bias
+        sc = scores(j, keys_of(c, j)) + bias
         top = jnp.max(sc, axis=0, keepdims=True)
         w = jnp.exp2(sc - top)
         run_max[j] = top
@@ -149,6 +163,8 @@
         for e in range(1, subs):
             image_side(cc, lax.rem(s + e, subs), e).wait_recv()
 
+    loads[5].wait()
+    loads[6].wait()
     seen_images = tokens[pl.ds(mine, 1), :]
     visible = jnp.zeros_like(seen_images)
     for i in range(lengths.shape[0]):
@@ -170,7 +186,7 @@
         put(cross_ref, j, out)
 
     def attend(b, j):
-        sc = scores(j, kv[b, j, 0])
+        sc = scores(j, keys_of(b, j))
         old = run_max[j]
         top = jnp.maximum(old, jnp.max(sc, axis=0, keepdims=True))
         w = jnp.exp2(sc - top)
@@ -185,23 +201,29 @@
         def _():
             finish(j)
 
-    @pl.loop(1, c + 1)
-    def _(t):
-        b = c - t
-        for i in range(share):
-            up(b, i).wait_recv()
+    def place(x):
+        return c - 1 - lax.div(x, heads), lax.rem(x, heads)
+
+    @pl.loop(0, c * heads + jnp.where(c > 0, 1, 0))
+    def _(x):
+        @pl.when(x < c * heads)
+        def _():
+            b, j = place(x)
+            up(b, j).wait_recv()
 
             @pl.when(c < n - 1)
             def _():
-                up(b, i).start()
+                up(b, j).start()
 
             for d in range(1, subs):
-                side(b, s * share + i, i, d).start()
-            attend(b, s * share + i)
+                side(b, j, s, d).start()
+
+        @pl.when(x > 0)
+        def _():
+            b, j = place(x - 1)
             for d in range(1, subs):
-                j = lax.rem(s + d, subs) * share + i
-                side(b, j, i, d).wait_recv()
-                attend(b, j)
+                side(b, j, lax.rem(s + d, subs), d).wait_recv()
+            attend(b, j)
 
     @pl.loop(1, n)
     def _(d):
@@ -216,14 +238,14 @@
     def _():
         @pl.loop(0, c + 1)
         def _(b):
-            for i in range(share):
-                up(b, i).wait_send()
+            for j in range(heads):
+                up(b, j).wait_send()
 
     @pl.loop(0, c)
     def _(b):
-        for i in range(share):
+        for j in range(heads):
             for d in range(1, subs):
-                side(b, s * share + i, i, d).wait_send()
+                side(b, j, s, d).wait_send()
 
 
 def local(queries, keys, values, image_keys, image_values, image_lengths, token_images):
@@ -232,38 +254,40 @@
     span, narrow = keys.shape
     heads, image_rows = narrow // HD, image_keys.shape[0]
     group = wide // narrow
-    share = heads // subs
     vmem = pl.BlockSpec(memory_space=pltpu.VMEM)
     hbm = pl.BlockSpec(memory_space=pl.ANY)
     dma = pltpu.SemaphoreType.DMA
     out = jax.ShapeDtypeStruct((rows, wide), jnp.bfloat16)
+    token_images = token_images.reshape(-1, rows)
     return pl.pallas_call(
         functools.partial(kernel, n, subs),
         out_shape=(out, out),
-        in_specs=[pl.BlockSpec(memory_space=pltpu.SMEM), vmem, hbm, hbm, hbm, hbm, hbm],
+        in_specs=[hbm] * 7,
         out_specs=(vmem, vmem),
         scratch_shapes=[
+            pltpu.SMEM(image_lengths.shape, jnp.int32),
+            pltpu.VMEM(token_images.shape, jnp.int32),
             pltpu.VMEM((rows, wide), jnp.bfloat16),
             pltpu.VMEM((span, narrow), jnp.bfloat16),
             pltpu.VMEM((span, narrow), jnp.bfloat16),
             pltpu.VMEM((heads, HD, group * rows), jnp.bfloat16),
-            pltpu.VMEM((n, heads, 2, span, HD), jnp.bfloat16),
+            pltpu.VMEM((n, heads, subs, 2, span // subs, HD), jnp.bfloat16),
             pltpu.VMEM((n * subs, 2, image_rows, narrow), jnp.bfloat16),
             pltpu.VMEM((heads, 1, group * rows), jnp.float32),
             pltpu.VMEM((heads, 1, group * rows), jnp.float32),
             pltpu.VMEM((heads, HD, group * rows), jnp.float32),
-            dma((5,)),
+            dma((7,)),
+            dma((n, heads, subs)),
             dma((n, heads)),
-            dma((n, share)),
-            dma((n, share, subs - 1)),
+            dma((n, heads, subs - 1)),
             dma((n * subs,)),
             dma((n - 1,)),
             dma((n, subs - 1)),
         ],
         compiler_params=pltpu.CompilerParams(
-            collective_id=0, has_side_effects=True, vmem_limit_bytes=40 * 1024 * 1024
+            collective_id=0, has_side_effects=True, vmem_limit_bytes=62 * 1024 * 1024
         ),
-    )(image_lengths, token_images.reshape(-1, rows), queries, keys, values, image_keys, image_values)
+    )(image_lengths, token_images, queries, keys, values, image_keys, image_values)
 
 
 def solution(mesh):

time: 33.7 us -> 29.3 us (0.87)
  local copies, waits for them, and re-layouts: 7.3 us -> 2.74 us
  Pallas kernels: 25.3 us -> 25.8 us
    unnamed x16 -> x4, local copies, waits for them, and re-layouts: 7.3 us -> 2.74 us
    pallas_call x1, Pallas kernels: 25.3 us -> 25.8 us  [local(): pl.pallas_call(functools.partial(kernel, n, subs), out_shape=(out, out),...]
where the time goes in v2:
time: 29.3 us; the launch traced here: 29.2 us
  Pallas kernels  25.8 us (88%)
  local copies, waits for them, and re-layouts  2.74 us (9%)
  between operations  0.65 us (2%)
    pallas_call x1, Pallas kernels, local(): pl.pallas_call(functools.partial(kernel, n, subs), out_shape=(out, out),...  25.8 us
    unnamed x4, local copies, waits for them, and re-layouts  2.74 us

profile of v2, /device:TPU:29, one launch (start us, length us, event | category | flops | bytes accessed | tf_op | source)
XLA Modules:
  0.0 29.2 jit_solution(3994190698396904879)
XLA Ops:
  0.6 25.8 %shard_map.86 = (bf16[128,2048]{1,0:T(8,128)(2,1)}, bf16[128,2048]{1,0:T(8,128)(2,1)}) custom-call(s32[8]{0:T(128)} %len_hbm.1, s32[8,128]{1,0:T(8,128)} %bitcast.1, bf16[128,2048]{1,0:T(8,128)(2,1)} %q_hbm.1, bf16[256,512]{1,0:T(8,128)(2,1)} %k_hbm.1, bf16[256,512]{1,0:T(8,128)(2,1)} %v_hbm.1, bf16[16,512]{1,0:T(8,128)(2,1)} %ik_hbm.1, bf16[16,512]{1,0:T(8,128)(2,1)} %iv_hbm.1), custom_call_target="tpu_custom_call" | custom-call | tf_op jit(solution)/shard_map/pallas_call | solution.py:262
  26.4 0.0 copy-start
  26.5 1.9 %copy.11 = bf16[128,2048]{1,0:T(8,128)(2,1)} copy(bf16[128,2048]{1,0:T(8,128)(2,1)} %get-tuple-element.4) | data formatting | bytes 1048576
  28.4 0.0 copy-done
  28.4 0.8 %copy.12 = bf16[128,2048]{1,0:T(8,128)(2,1)} copy(bf16[128,2048]{1,0:T(8,128)(2,1)S(1)} %copy-done) | data formatting | bytes 1048576
Async XLA Ops:
  26.4 2.0 %copy-start = (bf16[128,2048]{1,0:T(8,128)(2,1)S(1)}, bf16[128,2048]{1,0:T(8,128)(2,1)}, u32[]{:S(2)}) copy-start(bf16[128,2048]{1,0:T(8,128)(2,1)} %get-tuple-element.5) | copy-start | bytes 1572868

commit v3 on v2

--- a/solution.py
+++ b/solution.py
@@ -17,11 +17,16 @@
 def kernel(
     n, subs, len_hbm, tok_hbm, q_hbm, k_hbm, v_hbm, ik_hbm, iv_hbm, self_ref, cross_ref,
     lengths, tokens, q, k, v, qt, kv, img, run_max, run_sum, run_out,
-    in_sem, text_recv, up_send, side_send, img_recv, img_send, img_side,
+    guest_q, guest_max, guest_sum, guest_out, part_out, part_stats,
+    in_sem, text_recv, up_send, side_send, img_recv, img_up, img_down, img_side,
+    q_send, q_recv, part_send, part_recv,
 ):
     c, s = lax.axis_index("ctx"), lax.axis_index("sub")
     rows, span = q.shape[0], k.shape[0]
     heads = k.shape[1] // HD
+    guests = guest_q.shape[0]
+    kept = heads - guests
+    helper, last = c == n - 2, c == n - 1
     part = span // subs
     group = q.shape[1] // k.shape[1]
     image_rows = img.shape[2]
@@ -77,11 +82,34 @@
             device_id=sibling(d), device_id_type=MESH,
         )
 
-    def image_to(d):
-        return pltpu.make_async_remote_copy(
-            img.at[mine], img.at[mine], img_send.at[d - 1], img_recv.at[mine],
-            device_id={"ctx": lax.rem(c + d, n)}, device_id_type=MESH,
-        )
+    def image_up(cc):
+        at = cc * subs + s
+        return pltpu.make_async_remote_copy(
+            img.at[at], img.at[at], img_up.at[cc], img_recv.at[at],
+            device_id={"ctx": lax.rem(c + 1, n)}, device_id_type=MESH,
+        )
+
+    def image_down(cc):
+        at = cc * subs + s
+        return pltpu.make_async_remote_copy(
+            img.at[at], img.at[at], img_down.at[cc], img_recv.at[at],
+            device_id={"ctx": lax.rem(c + n - 1, n)}, device_id_type=MESH,
+        )
+
+    def query_down(i):
+        return pltpu.make_async_remote_copy(
+            qt.at[kept + i], guest_q.at[i], q_send.at[i], q_recv.at[i],
+            device_id={"ctx": lax.rem(c + n - 1, n)}, device_id_type=MESH,
+        )
+
+    def part_up(i):
+        return [
+            pltpu.make_async_remote_copy(
+                ref.at[i], ref.at[i], part_send.at[i, e], part_recv.at[i, e],
+                device_id={"ctx": lax.rem(c + 1, n)}, device_id_type=MESH,
+            )
+            for e, ref in enumerate([part_stats, part_out])
+        ]
 
     def image_side(cc, ss, d):
         at = cc * subs + ss
@@ -90,17 +118,18 @@
             device_id=sibling(d), device_id_type=MESH,
         )
 
-    @pl.loop(1, n)
-    def _(d):
-        image_to(d).start()
+    @pl.when(c < n - 1)
+    def _():
+        image_up(c).start()
+        for j in range(kept):
+            up(c, j).start()
+
+    @pl.when(c > 0)
+    def _():
+        image_down(c).start()
 
     for d in range(1, subs):
         image_side(c, s, d).start()
-
-    @pl.when(c < n - 1)
-    def _():
-        for j in range(heads):
-            up(c, j).start()
 
     for d in range(1, subs):
         lay_out(lax.rem(s + d, subs))
@@ -110,8 +139,13 @@
             h = j * group + g
             qt[j, :, g * rows:(g + 1) * rows] = q[:, h * HD:(h + 1) * HD].T
 
-    def scores(j, key_rows):
-        return jnp.dot(key_rows, qt[j], preferred_element_type=jnp.float32) * SCALE
+    @pl.when(last)
+    def _():
+        for i in range(guests):
+            query_down(i).start()
+
+    def scores(query, key_rows):
+        return jnp.dot(key_rows, query, preferred_element_type=jnp.float32) * SCALE
 
     def wide(x):
         return jnp.concatenate([x] * group, axis=1)
@@ -135,28 +169,161 @@
     def finish(j):
         put(self_ref, j, run_out[j] * (1.0 / run_sum[j]))
 
+    def image_step(d):
+        @pl.when(c >= d)
+        def _():
+            cc = c - d
+            image_up(cc).wait_recv()
+
+            @pl.when(c < n - 1)
+            def _():
+                image_up(cc).start()
+
+            for e in range(1, subs):
+                image_side(cc, s, e).start()
+
+        @pl.when(c + d < n)
+        def _():
+            cc = c + d
+            image_down(cc).wait_recv()
+
+            @pl.when(c > 0)
+            def _():
+                image_down(cc).start()
+
+            for e in range(1, subs):
+                image_side(cc, s, e).start()
+
     key_at = lax.broadcasted_iota(jnp.int32, (span, rows), 0)
     row_at = lax.broadcasted_iota(jnp.int32, (span, rows), 1) + s * rows
     bias = wide(jnp.where(key_at <= row_at, 0.0, LOW))
     for j in range(heads):
-        sc = scores(j, keys_of(c, j)) + bias
+        sc = scores(qt[j], keys_of(c, j)) + bias
         top = jnp.max(sc, axis=0, keepdims=True)
         w = jnp.exp2(sc - top)
         run_max[j] = top
         run_sum[j] = jnp.sum(w, axis=0, keepdims=True)
         run_out[j] = jnp.dot(values_of(c, j), w.astype(jnp.bfloat16), preferred_element_type=jnp.float32)
+        if j + 1 < n:
+            image_step(j + 1)
+
+    if heads + 1 < n:
+        @pl.loop(heads + 1, n)
+        def _(d):
+            image_step(d)
 
     @pl.when(c == 0)
     def _():
         for j in range(heads):
             finish(j)
 
-    @pl.loop(1, n)
-    def _(d):
-        cc = lax.rem(c + d, n)
-        image_side(cc, s, 1).wait_recv()
-        for e in range(1, subs):
-            image_side(cc, s, e).start()
+    def update(key_rows, value_cols, query, maxes, sums, outs, i):
+        sc = scores(query, key_rows)
+        old = maxes[i]
+        top = jnp.maximum(old, jnp.max(sc, axis=0, keepdims=True))
+        w = jnp.exp2(sc - top)
+        factor = jnp.exp2(old - top)
+        maxes[i] = top
+        sums[i] = sums[i] * factor + jnp.sum(w, axis=0, keepdims=True)
+        outs[i] = outs[i] * factor + jnp.dot(
+            value_cols, w.astype(jnp.bfloat16), preferred_element_type=jnp.float32
+        )
+
+    def attend(b, j):
+        update(keys_of(b, j), values_of(b, j), qt[j], run_max, run_sum, run_out, j)
+
+        @pl.when(b == 0)
+        def _():
+            finish(j)
+
+    def attend_guest(b, i):
+        j = kept + i
+        update(keys_of(b, j), values_of(b, j), guest_q[i], guest_max, guest_sum, guest_out, i)
+
+        @pl.when(b == 0)
+        def _():
+            part_out[i] = (guest_out[i] * (1.0 / guest_sum[i])).astype(jnp.bfloat16)
+            part_stats[i, 0:1] = guest_max[i]
+            part_stats[i, 1:2] = guest_sum[i]
+            for copy in part_up(i):
+                copy.start()
+
+    def await_siblings(b, j):
+        for d in range(1, subs):
+            side(b, j, lax.rem(s + d, subs), d).wait_recv()
+
+    def pass_on(b, j, onward):
+        up(b, j).wait_recv()
+
+        @pl.when(onward)
+        def _():
+            up(b, j).start()
+
+        for d in range(1, subs):
+            side(b, j, s, d).start()
+
+    def place(x):
+        return c - 1 - lax.div(x, kept), lax.rem(x, kept)
+
+    @pl.loop(0, c * kept + jnp.where(c > 0, 1, 0))
+    def _(x):
+        @pl.when(x < c * kept)
+        def _():
+            pass_on(*place(x), c < n - 1)
+
+        @pl.when(x > 0)
+        def _():
+            b, j = place(x - 1)
+            await_siblings(b, j)
+            attend(b, j)
+
+    @pl.when(c < n - 2)
+    def _():
+        up(c, kept).start()
+
+    @pl.when(helper)
+    def _():
+        for i in range(guests):
+            query_down(i).wait_recv()
+            guest_max[i] = jnp.full(guest_max.shape[1:], LOW, jnp.float32)
+            guest_sum[i] = jnp.zeros(guest_sum.shape[1:], jnp.float32)
+            guest_out[i] = jnp.zeros(guest_out.shape[1:], jnp.float32)
+            attend_guest(c, i)
+
+    @pl.when(jnp.logical_and(c == 0, c < n - 2))
+    def _():
+        for i in range(1, guests):
+            up(c, kept + i).start()
+
+    turns = jnp.where(last, 0, c * guests)
+
+    def guest_place(y):
+        return c - 1 - lax.rem(y, jnp.maximum(c, 1)), lax.div(y, jnp.maximum(c, 1))
+
+    @pl.loop(0, turns + jnp.where(turns > 0, 1, 0))
+    def _(y):
+        @pl.when(y < turns)
+        def _():
+            b, i = guest_place(y)
+            pass_on(b, kept + i, c < n - 2)
+
+            @pl.when(jnp.logical_and(c < n - 2, jnp.logical_and(b == 0, i + 1 < guests)))
+            def _():
+                up(c, kept + i + 1).start()
+
+        @pl.when(y > 0)
+        def _():
+            b, i = guest_place(y - 1)
+            attend(b, kept + i)
+
+        @pl.when(y < turns)
+        def _():
+            b, i = guest_place(y)
+            await_siblings(b, kept + i)
+
+            @pl.when(helper)
+            def _():
+                attend_guest(b, i)
 
     @pl.loop(0, n)
     def _(cc):
@@ -174,7 +341,7 @@
     allowed = lax.broadcasted_iota(jnp.int32, (count, group * rows), 0) < visible
     for j in range(heads):
         cols = slice(j * HD, (j + 1) * HD)
-        sc = jnp.where(allowed, scores(j, img[:, 0, :, cols].reshape(count, HD)), LOW)
+        sc = jnp.where(allowed, scores(qt[j], img[:, 0, :, cols].reshape(count, HD)), LOW)
         top = jnp.max(sc, axis=0, keepdims=True)
         w = jnp.where(allowed, jnp.exp2(sc - top), 0.0)
         total = jnp.sum(w, axis=0, keepdims=True)
@@ -185,67 +352,54 @@
         out = jnp.where(visible > 0, out * (1.0 / jnp.where(visible > 0, total, 1.0)), 0.0)
         put(cross_ref, j, out)
 
-    def attend(b, j):
-        sc = scores(j, keys_of(b, j))
-        old = run_max[j]
-        top = jnp.maximum(old, jnp.max(sc, axis=0, keepdims=True))
-        w = jnp.exp2(sc - top)
-        factor = jnp.exp2(old - top)
-        run_max[j] = top
-        run_sum[j] = run_sum[j] * factor + jnp.sum(w, axis=0, keepdims=True)
-        run_out[j] = run_out[j] * factor + jnp.dot(
-            values_of(b, j), w.astype(jnp.bfloat16), preferred_element_type=jnp.float32
-        )
-
-        @pl.when(b == 0)
-        def _():
-            finish(j)
-
-    def place(x):
-        return c - 1 - lax.div(x, heads), lax.rem(x, heads)
-
-    @pl.loop(0, c * heads + jnp.where(c > 0, 1, 0))
-    def _(x):
-        @pl.when(x < c * heads)
-        def _():
-            b, j = place(x)
-            up(b, j).wait_recv()
-
-            @pl.when(c < n - 1)
-            def _():
-                up(b, j).start()
-
-            for d in range(1, subs):
-                side(b, j, s, d).start()
-
-        @pl.when(x > 0)
-        def _():
-            b, j = place(x - 1)
-            for d in range(1, subs):
-                side(b, j, lax.rem(s + d, subs), d).wait_recv()
-            attend(b, j)
-
-    @pl.loop(1, n)
-    def _(d):
-        image_to(d).wait_send()
+    @pl.when(last)
+    def _():
+        for i in range(guests):
+            j = kept + i
+            for copy in part_up(i):
+                copy.wait_recv()
+            their_max, their_sum = part_stats[i, 0:1], part_stats[i, 1:2]
+            top = jnp.maximum(run_max[j], their_max)
+            factor = jnp.exp2(run_max[j] - top)
+            weight = their_sum * jnp.exp2(their_max - top)
+            scale = 1.0 / (run_sum[j] * factor + weight)
+            out = run_out[j] * (factor * scale) + part_out[i].astype(jnp.float32) * (weight * scale)
+            put(self_ref, j, out)
 
     @pl.loop(0, n)
     def _(cc):
+        @pl.when(jnp.logical_and(cc <= c, c < n - 1))
+        def _():
+            image_up(cc).wait_send()
+
+        @pl.when(jnp.logical_and(cc >= c, c > 0))
+        def _():
+            image_down(cc).wait_send()
+
         for d in range(1, subs):
             image_side(cc, s, d).wait_send()
 
-    @pl.when(c < n - 1)
-    def _():
-        @pl.loop(0, c + 1)
-        def _(b):
-            for j in range(heads):
-                up(b, j).wait_send()
-
-    @pl.loop(0, c)
+    @pl.loop(0, c + 1)
     def _(b):
         for j in range(heads):
-            for d in range(1, subs):
-                side(b, j, s, d).wait_send()
+            @pl.when(c < (n - 1 if j < kept else n - 2))
+            def _():
+                up(b, j).wait_send()
+
+            @pl.when(jnp.logical_and(b < c, c < (n if j < kept else n - 1)))
+            def _():
+                for d in range(1, subs):
+                    side(b, j, s, d).wait_send()
+
+    for i in range(guests):
+        @pl.when(last)
+        def _():
+            query_down(i).wait_send()
+
+        @pl.when(helper)
+        def _():
+            for copy in part_up(i):
+                copy.wait_send()
 
 
 def local(queries, keys, values, image_keys, image_values, image_lengths, token_images):
@@ -254,10 +408,11 @@
     span, narrow = keys.shape
     heads, image_rows = narrow // HD, image_keys.shape[0]
     group = wide // narrow
+    guests = heads // 2
     vmem = pl.BlockSpec(memory_space=pltpu.VMEM)
-    hbm = pl.BlockSpec(memory_space=pl.ANY)
+    hbm = pl.BlockSpec(memory_space=pltpu.HBM)
     dma = pltpu.SemaphoreType.DMA
-    out = jax.ShapeDtypeStruct((rows, wide), jnp.bfloat16)
+    out = pltpu.VMEM((rows, wide), jnp.bfloat16)
     token_images = token_images.reshape(-1, rows)
     return pl.pallas_call(
         functools.partial(kernel, n, subs),
@@ -276,16 +431,27 @@
             pltpu.VMEM((heads, 1, group * rows), jnp.float32),
             pltpu.VMEM((heads, 1, group * rows), jnp.float32),
             pltpu.VMEM((heads, HD, group * rows), jnp.float32),
+            pltpu.VMEM((guests, HD, group * rows), jnp.bfloat16),
+            pltpu.VMEM((guests, 1, group * rows), jnp.float32),
+            pltpu.VMEM((guests, 1, group * rows), jnp.float32),
+            pltpu.VMEM((guests, HD, group * rows), jnp.float32),
+            pltpu.VMEM((guests, HD, group * rows), jnp.bfloat16),
+            pltpu.VMEM((guests, 2, group * rows), jnp.float32),
             dma((7,)),
             dma((n, heads, subs)),
             dma((n, heads)),
             dma((n, heads, subs - 1)),
             dma((n * subs,)),
-            dma((n - 1,)),
+            dma((n,)),
+            dma((n,)),
             dma((n, subs - 1)),
+            dma((guests,)),
+            dma((guests,)),
+            dma((guests, 2)),
+            dma((guests, 2)),
         ],
         compiler_params=pltpu.CompilerParams(
-            collective_id=0, has_side_effects=True, vmem_limit_bytes=62 * 1024 * 1024
+            collective_id=0, has_side_effects=True, vmem_limit_bytes=60 * 1024 * 1024
         ),
     )(image_lengths, token_images, queries, keys, values, image_keys, image_values)
 

time: 29.3 us -> 31.2 us (1.065)
  Pallas kernels: 25.8 us -> 28.8 us
  local copies, waits for them, and re-layouts: 2.74 us -> 1.59 us
    pallas_call x1, Pallas kernels: 25.8 us -> 28.8 us  [local(): pl.pallas_call(functools.partial(kernel, n, subs), out_shape=(out, out),...]
    unnamed x4 -> x2, local copies, waits for them, and re-layouts: 2.74 us -> 1.59 us
where the time goes in v3:
time: 31.2 us; the launch traced here: 31 us
  Pallas kernels  28.8 us (92%)
  local copies, waits for them, and re-layouts  1.59 us (5%)
  between operations  0.64 us (2%)
    pallas_call x1, Pallas kernels, local(): pl.pallas_call(functools.partial(kernel, n, subs), out_shape=(out, out),...  28.8 us
    unnamed x2, local copies, waits for them, and re-layouts  1.59 us

profile of v3, /device:TPU:29, one launch (start us, length us, event | category | flops | bytes accessed | tf_op | source)
XLA Modules:
  0.0 31.0 jit_solution(1836687319001537062)
XLA Ops:
  0.6 28.8 %shard_map.86 = (bf16[128,2048]{1,0:T(8,128)(2,1)S(1)}, bf16[128,2048]{1,0:T(8,128)(2,1)S(1)}) custom-call(s32[8]{0:T(128)} %len_hbm.1, s32[8,128]{1,0:T(8,128)} %bitcast.1, bf16[128,2048]{1,0:T(8,128)(2,1)} %q_hbm.1, bf16[256,512]{1,0:T(8,128)(2,1)} %k_hbm.1, bf16[256,512]{1,0:T(8,128)(2,1)} %v_hbm.1, bf16[16,512]{1,0:T(8,128)(2,1)} %ik_hbm.1, ...), custom_call_target="tpu_custom_call" | custom-call | tf_op jit(solution)/shard_map/pallas_call | solution.py:417
  29.4 0.8 %copy.11 = bf16[128,2048]{1,0:T(8,128)(2,1)} copy(bf16[128,2048]{1,0:T(8,128)(2,1)S(1)} %get-tuple-element.2) | data formatting | bytes 1048576
  30.2 0.8 %copy.12 = bf16[128,2048]{1,0:T(8,128)(2,1)} copy(bf16[128,2048]{1,0:T(8,128)(2,1)S(1)} %get-tuple-element.3) | data formatting | bytes 1048576

commit v4 on v2

--- a/solution.py
+++ b/solution.py
@@ -138,13 +138,19 @@
     key_at = lax.broadcasted_iota(jnp.int32, (span, rows), 0)
     row_at = lax.broadcasted_iota(jnp.int32, (span, rows), 1) + s * rows
     bias = wide(jnp.where(key_at <= row_at, 0.0, LOW))
-    for j in range(heads):
-        sc = scores(j, keys_of(c, j)) + bias
-        top = jnp.max(sc, axis=0, keepdims=True)
-        w = jnp.exp2(sc - top)
-        run_max[j] = top
-        run_sum[j] = jnp.sum(w, axis=0, keepdims=True)
-        run_out[j] = jnp.dot(values_of(c, j), w.astype(jnp.bfloat16), preferred_element_type=jnp.float32)
+    batch = 2 if heads % 2 == 0 else 1
+    for first in range(0, heads, batch):
+        js = range(first, first + batch)
+        scs = [scores(j, keys_of(c, j)) + bias for j in js]
+        tops = [jnp.max(sc, axis=0, keepdims=True) for sc in scs]
+        ws = [jnp.exp2(sc - top) for sc, top in zip(scs, tops)]
+        sums = [jnp.sum(w, axis=0, keepdims=True) for w in ws]
+        outs = [
+            jnp.dot(values_of(c, j), w.astype(jnp.bfloat16), preferred_element_type=jnp.float32)
+            for j, w in zip(js, ws)
+        ]
+        for j, top, total, out in zip(js, tops, sums, outs):
+            run_max[j], run_sum[j], run_out[j] = top, total, out
 
     @pl.when(c == 0)
     def _():
@@ -185,45 +191,74 @@
         out = jnp.where(visible > 0, out * (1.0 / jnp.where(visible > 0, total, 1.0)), 0.0)
         put(cross_ref, j, out)
 
-    def attend(b, j):
-        sc = scores(j, keys_of(b, j))
-        old = run_max[j]
-        top = jnp.maximum(old, jnp.max(sc, axis=0, keepdims=True))
-        w = jnp.exp2(sc - top)
-        factor = jnp.exp2(old - top)
-        run_max[j] = top
-        run_sum[j] = run_sum[j] * factor + jnp.sum(w, axis=0, keepdims=True)
-        run_out[j] = run_out[j] * factor + jnp.dot(
-            values_of(b, j), w.astype(jnp.bfloat16), preferred_element_type=jnp.float32
-        )
+    def attend(b, first):
+        js = [first + i for i in range(batch)]
+        olds, totals, accs = [run_max[j] for j in js], [run_sum[j] for j in js], [run_out[j] for j in js]
+        scs = [scores(j, keys_of(b, j)) for j in js]
+        cols = [values_of(b, j) for j in js]
+        tops = [jnp.maximum(old, jnp.max(sc, axis=0, keepdims=True)) for old, sc in zip(olds, scs)]
+        ws = [jnp.exp2(sc - top) for sc, top in zip(scs, tops)]
+        factors = [jnp.exp2(old - top) for old, top in zip(olds, tops)]
+        totals = [
+            total * factor + jnp.sum(w, axis=0, keepdims=True)
+            for total, factor, w in zip(totals, factors, ws)
+        ]
+        accs = [
+            acc * factor + jnp.dot(col, w.astype(jnp.bfloat16), preferred_element_type=jnp.float32)
+            for acc, factor, col, w in zip(accs, factors, cols, ws)
+        ]
+
+        @pl.when(b > 0)
+        def _():
+            for j, top, total, acc in zip(js, tops, totals, accs):
+                run_max[j], run_sum[j], run_out[j] = top, total, acc
 
         @pl.when(b == 0)
         def _():
-            finish(j)
+            for j, total, acc in zip(js, totals, accs):
+                put(self_ref, j, acc * (1.0 / total))
+
+    turns = c * heads // batch
 
     def place(x):
-        return c - 1 - lax.div(x, heads), lax.rem(x, heads)
-
-    @pl.loop(0, c * heads + jnp.where(c > 0, 1, 0))
-    def _(x):
-        @pl.when(x < c * heads)
-        def _():
-            b, j = place(x)
-            up(b, j).wait_recv()
+        return c - 1 - lax.div(x * batch, heads), lax.rem(x * batch, heads)
+
+    def receive(x):
+        b, first = place(x)
+        for i in range(batch):
+            up(b, first + i).wait_recv()
 
             @pl.when(c < n - 1)
             def _():
-                up(b, j).start()
+                up(b, first + i).start()
 
             for d in range(1, subs):
-                side(b, j, s, d).start()
-
-        @pl.when(x > 0)
+                side(b, first + i, s, d).start()
+
+    def consume(x):
+        b, first = place(x)
+        for i in range(batch):
+            for d in range(1, subs):
+                side(b, first + i, lax.rem(s + d, subs), d).wait_recv()
+        attend(b, first)
+
+    @pl.when(c > 0)
+    def _():
+        @pl.when(turns > 1)
         def _():
-            b, j = place(x - 1)
-            for d in range(1, subs):
-                side(b, j, lax.rem(s + d, subs), d).wait_recv()
-            attend(b, j)
+            receive(jnp.int32(0))
+
+        @pl.loop(1, turns - 1)
+        def _(x):
+            receive(x)
+            consume(x - 1)
+
+        @pl.when(turns > 1)
+        def _():
+            consume(turns - 2)
+
+        receive(turns - 1)
+        consume(turns - 1)
 
     @pl.loop(1, n)
     def _(d):
@@ -255,9 +290,9 @@
     heads, image_rows = narrow // HD, image_keys.shape[0]
     group = wide // narrow
     vmem = pl.BlockSpec(memory_space=pltpu.VMEM)
-    hbm = pl.BlockSpec(memory_space=pl.ANY)
+    hbm = pl.BlockSpec(memory_space=pltpu.HBM)
     dma = pltpu.SemaphoreType.DMA
-    out = jax.ShapeDtypeStruct((rows, wide), jnp.bfloat16)
+    out = pltpu.VMEM((rows, wide), jnp.bfloat16)
     token_images = token_images.reshape(-1, rows)
     return pl.pallas_call(
         functools.partial(kernel, n, subs),
@@ -285,7 +320,7 @@
             dma((n, subs - 1)),
         ],
         compiler_params=pltpu.CompilerParams(
-            collective_id=0, has_side_effects=True, vmem_limit_bytes=62 * 1024 * 1024
+            collective_id=0, has_side_effects=True, vmem_limit_bytes=60 * 1024 * 1024
         ),
     )(image_lengths, token_images, queries, keys, values, image_keys, image_values)
 

time: 29.3 us -> 27.4 us (0.935)
  local copies, waits for them, and re-layouts: 2.74 us -> 1.59 us
  Pallas kernels: 25.8 us -> 25 us
    unnamed x4 -> x2, local copies, waits for them, and re-layouts: 2.74 us -> 1.59 us
    pallas_call x1, Pallas kernels: 25.8 us -> 25 us  [local(): pl.pallas_call(functools.partial(kernel, n, subs), out_shape=(out, out),...]
where the time goes in v4:
time: 27.4 us; the launch traced here: 27.3 us
  Pallas kernels  25 us (91%)
  local copies, waits for them, and re-layouts  1.59 us (6%)
  between operations  0.64 us (2%)
    pallas_call x1, Pallas kernels, local(): pl.pallas_call(functools.partial(kernel, n, subs), out_shape=(out, out),...  25 us
    unnamed x2, local copies, waits for them, and re-layouts  1.59 us

profile of v4, /device:TPU:29, one launch (start us, length us, event | category | flops | bytes accessed | tf_op | source)
XLA Modules:
  0.0 27.3 jit_solution(10607649482440970621)
XLA Ops:
  0.6 25.0 %shard_map.86 = (bf16[128,2048]{1,0:T(8,128)(2,1)S(1)}, bf16[128,2048]{1,0:T(8,128)(2,1)S(1)}) custom-call(s32[8]{0:T(128)} %len_hbm.1, s32[8,128]{1,0:T(8,128)} %bitcast.1, bf16[128,2048]{1,0:T(8,128)(2,1)} %q_hbm.1, bf16[256,512]{1,0:T(8,128)(2,1)} %k_hbm.1, bf16[256,512]{1,0:T(8,128)(2,1)} %v_hbm.1, bf16[16,512]{1,0:T(8,128)(2,1)} %ik_hbm.1, ...), custom_call_target="tpu_custom_call" | custom-call | tf_op jit(solution)/shard_map/pallas_call | solution.py:297
  25.7 0.8 %copy.11 = bf16[128,2048]{1,0:T(8,128)(2,1)} copy(bf16[128,2048]{1,0:T(8,128)(2,1)S(1)} %get-tuple-element.2) | data formatting | bytes 1048576
  26.5 0.8 %copy.12 = bf16[128,2048]{1,0:T(8,128)(2,1)} copy(bf16[128,2048]{1,0:T(8,128)(2,1)S(1)} %get-tuple-element.3) | data formatting | bytes 1048576

commit v5 on v4

--- a/solution.py
+++ b/solution.py
@@ -168,6 +168,46 @@
     def _(cc):
         for e in range(1, subs):
             image_side(cc, lax.rem(s + e, subs), e).wait_recv()
+
+    turns = c * heads // batch
+
+    def place(x):
+        return c - 1 - lax.div(x * batch, heads), lax.rem(x * batch, heads)
+
+    def receive_head(b, j):
+        up(b, j).wait_recv()
+
+        @pl.when(c < n - 1)
+        def _():
+            up(b, j).start()
+
+        for d in range(1, subs):
+            side(b, j, s, d).start()
+
+    def await_siblings(b, j):
+        for d in range(1, subs):
+            side(b, j, lax.rem(s + d, subs), d).wait_recv()
+
+    def receive(x):
+        b, first = place(x)
+        for i in range(batch):
+            receive_head(b, first + i)
+
+    def consume(x):
+        b, first = place(x)
+        js = [first + i for i in range(batch)]
+        for j in js:
+            await_siblings(b, j)
+        attend([(j, keys_of(b, j), values_of(b, j)) for j in js])
+
+        @pl.when(b == 0)
+        def _():
+            for j in js:
+                finish(j)
+
+    @pl.when(turns > 1)
+    def _():
+        receive(jnp.int32(0))
 
     loads[5].wait()
     loads[6].wait()
@@ -191,11 +231,10 @@
         out = jnp.where(visible > 0, out * (1.0 / jnp.where(visible > 0, total, 1.0)), 0.0)
         put(cross_ref, j, out)
 
-    def attend(b, first):
-        js = [first + i for i in range(batch)]
+    def attend(items):
+        js = [j for j, _, _ in items]
         olds, totals, accs = [run_max[j] for j in js], [run_sum[j] for j in js], [run_out[j] for j in js]
-        scs = [scores(j, keys_of(b, j)) for j in js]
-        cols = [values_of(b, j) for j in js]
+        scs = [scores(j, key_rows) for j, key_rows, _ in items]
         tops = [jnp.maximum(old, jnp.max(sc, axis=0, keepdims=True)) for old, sc in zip(olds, scs)]
         ws = [jnp.exp2(sc - top) for sc, top in zip(scs, tops)]
         factors = [jnp.exp2(old - top) for old, top in zip(olds, tops)]
@@ -204,50 +243,18 @@
             for total, factor, w in zip(totals, factors, ws)
         ]
         accs = [
-            acc * factor + jnp.dot(col, w.astype(jnp.bfloat16), preferred_element_type=jnp.float32)
-            for acc, factor, col, w in zip(accs, factors, cols, ws)
+            acc * factor + jnp.dot(cols, w.astype(jnp.bfloat16), preferred_element_type=jnp.float32)
+            for acc, factor, (_, _, cols), w in zip(accs, factors, items, ws)
         ]
-
-        @pl.when(b > 0)
-        def _():
-            for j, top, total, acc in zip(js, tops, totals, accs):
-                run_max[j], run_sum[j], run_out[j] = top, total, acc
-
-        @pl.when(b == 0)
-        def _():
-            for j, total, acc in zip(js, totals, accs):
-                put(self_ref, j, acc * (1.0 / total))
-
-    turns = c * heads // batch
-
-    def place(x):
-        return c - 1 - lax.div(x * batch, heads), lax.rem(x * batch, heads)
-
-    def receive(x):
-        b, first = place(x)
-        for i in range(batch):
-            up(b, first + i).wait_recv()
-
-            @pl.when(c < n - 1)
-            def _():
-                up(b, first + i).start()
-
-            for d in range(1, subs):
-                side(b, first + i, s, d).start()
-
-    def consume(x):
-        b, first = place(x)
-        for i in range(batch):
-            for d in range(1, subs):
-                side(b, first + i, lax.rem(s + d, subs), d).wait_recv()
-        attend(b, first)
+        for j, top, total, acc in zip(js, tops, totals, accs):
+            run_max[j], run_sum[j], run_out[j] = top, total, acc
+
+    def attend_part(b, j, ss):
+        cols = jnp.concatenate([kv[b, j, ss, 1, i:i + HD] for i in range(0, part, HD)], axis=1)
+        attend([(j, kv[b, j, ss, 0], cols)])
 
     @pl.when(c > 0)
     def _():
-        @pl.when(turns > 1)
-        def _():
-            receive(jnp.int32(0))
-
         @pl.loop(1, turns - 1)
         def _(x):
             receive(x)
@@ -257,8 +264,16 @@
         def _():
             consume(turns - 2)
 
-        receive(turns - 1)
-        consume(turns - 1)
+        b, first = place(turns - 1)
+        for i in range(batch):
+            receive_head(b, first + i)
+            if i > 0:
+                finish(first + i - 1)
+            attend_part(b, first + i, s)
+            await_siblings(b, first + i)
+            for d in range(1, subs):
+                attend_part(b, first + i, lax.rem(s + d, subs))
+        finish(first + batch - 1)
 
     @pl.loop(1, n)
     def _(d):

time: 27.4 us -> 27 us (0.985)
  Pallas kernels: 25 us -> 24.6 us
    pallas_call x1, Pallas kernels: 25 us -> 24.6 us  [local(): pl.pallas_call(functools.partial(kernel, n, subs), out_shape=(out, out),...]
where the time goes in v5:
time: 27 us; the launch traced here: 26.8 us
  Pallas kernels  24.6 us (91%)
  local copies, waits for them, and re-layouts  1.59 us (6%)
  between operations  0.64 us (2%)
    pallas_call x1, Pallas kernels, local(): pl.pallas_call(functools.partial(kernel, n, subs), out_shape=(out, out),...  24.6 us
    unnamed x2, local copies, waits for them, and re-layouts  1.59 us

profile of v5, /device:TPU:29, one launch (start us, length us, event | category | flops | bytes accessed | tf_op | source)
XLA Modules:
  0.0 26.8 jit_solution(4213841033266634225)
XLA Ops:
  0.6 24.6 %shard_map.86 = (bf16[128,2048]{1,0:T(8,128)(2,1)S(1)}, bf16[128,2048]{1,0:T(8,128)(2,1)S(1)}) custom-call(s32[8]{0:T(128)} %len_hbm.1, s32[8,128]{1,0:T(8,128)} %bitcast.1, bf16[128,2048]{1,0:T(8,128)(2,1)} %q_hbm.1, bf16[256,512]{1,0:T(8,128)(2,1)} %k_hbm.1, bf16[256,512]{1,0:T(8,128)(2,1)} %v_hbm.1, bf16[16,512]{1,0:T(8,128)(2,1)} %ik_hbm.1, ...), custom_call_target="tpu_custom_call" | custom-call | tf_op jit(solution)/shard_map/pallas_call | solution.py:312
  25.2 0.8 %copy.11 = bf16[128,2048]{1,0:T(8,128)(2,1)} copy(bf16[128,2048]{1,0:T(8,128)(2,1)S(1)} %get-tuple-element.2) | data formatting | bytes 1048576
  26.0 0.8 %copy.12 = bf16[128,2048]{1,0:T(8,128)(2,1)} copy(bf16[128,2048]{1,0:T(8,128)(2,1)S(1)} %get-tuple-element.3) | data formatting | bytes 1048576

commit v6 on v5

--- a/solution.py
+++ b/solution.py
@@ -110,11 +110,10 @@
             h = j * group + g
             qt[j, :, g * rows:(g + 1) * rows] = q[:, h * HD:(h + 1) * HD].T
 
-    def scores(j, key_rows):
-        return jnp.dot(key_rows, qt[j], preferred_element_type=jnp.float32) * SCALE
-
-    def wide(x):
-        return jnp.concatenate([x] * group, axis=1)
+    tiles = [slice(g * rows, (g + 1) * rows) for g in range(group)]
+
+    def scores(j, key_rows, cols):
+        return jnp.dot(key_rows, qt[j, :, cols], preferred_element_type=jnp.float32) * SCALE
 
     def put(ref, j, out):
         out = out.astype(jnp.bfloat16)
@@ -137,20 +136,21 @@
 
     key_at = lax.broadcasted_iota(jnp.int32, (span, rows), 0)
     row_at = lax.broadcasted_iota(jnp.int32, (span, rows), 1) + s * rows
-    bias = wide(jnp.where(key_at <= row_at, 0.0, LOW))
+    bias = jnp.where(key_at <= row_at, 0.0, LOW)
     batch = 2 if heads % 2 == 0 else 1
     for first in range(0, heads, batch):
         js = range(first, first + batch)
-        scs = [scores(j, keys_of(c, j)) + bias for j in js]
-        tops = [jnp.max(sc, axis=0, keepdims=True) for sc in scs]
-        ws = [jnp.exp2(sc - top) for sc, top in zip(scs, tops)]
-        sums = [jnp.sum(w, axis=0, keepdims=True) for w in ws]
-        outs = [
-            jnp.dot(values_of(c, j), w.astype(jnp.bfloat16), preferred_element_type=jnp.float32)
-            for j, w in zip(js, ws)
-        ]
-        for j, top, total, out in zip(js, tops, sums, outs):
-            run_max[j], run_sum[j], run_out[j] = top, total, out
+        for cols in tiles:
+            scs = [scores(j, keys_of(c, j), cols) + bias for j in js]
+            tops = [jnp.max(sc, axis=0, keepdims=True) for sc in scs]
+            ws = [jnp.exp2(sc - top) for sc, top in zip(scs, tops)]
+            sums = [jnp.sum(w, axis=0, keepdims=True) for w in ws]
+            outs = [
+                jnp.dot(values_of(c, j), w.astype(jnp.bfloat16), preferred_element_type=jnp.float32)
+                for j, w in zip(js, ws)
+            ]
+            for j, top, total, out in zip(js, tops, sums, outs):
+                run_max[j, :, cols], run_sum[j, :, cols], run_out[j, :, cols] = top, total, out
 
     @pl.when(c == 0)
     def _():
@@ -215,39 +215,42 @@
     visible = jnp.zeros_like(seen_images)
     for i in range(lengths.shape[0]):
         visible = visible + jnp.where(seen_images > i, lengths[i], 0)
-    visible = wide(visible)
     count = n * subs * image_rows
-    allowed = lax.broadcasted_iota(jnp.int32, (count, group * rows), 0) < visible
+    allowed = lax.broadcasted_iota(jnp.int32, (count, rows), 0) < visible
     for j in range(heads):
-        cols = slice(j * HD, (j + 1) * HD)
-        sc = jnp.where(allowed, scores(j, img[:, 0, :, cols].reshape(count, HD)), LOW)
-        top = jnp.max(sc, axis=0, keepdims=True)
-        w = jnp.where(allowed, jnp.exp2(sc - top), 0.0)
-        total = jnp.sum(w, axis=0, keepdims=True)
-        out = jnp.dot(
-            img[:, 1, :, cols].reshape(count, HD).T, w.astype(jnp.bfloat16),
-            preferred_element_type=jnp.float32,
-        )
-        out = jnp.where(visible > 0, out * (1.0 / jnp.where(visible > 0, total, 1.0)), 0.0)
-        put(cross_ref, j, out)
+        head = slice(j * HD, (j + 1) * HD)
+        image_k = img[:, 0, :, head].reshape(count, HD)
+        image_vt = img[:, 1, :, head].reshape(count, HD).T
+        for g, cols in enumerate(tiles):
+            sc = jnp.where(allowed, scores(j, image_k, cols), LOW)
+            top = jnp.max(sc, axis=0, keepdims=True)
+            w = jnp.where(allowed, jnp.exp2(sc - top), 0.0)
+            total = jnp.sum(w, axis=0, keepdims=True)
+            out = jnp.dot(image_vt, w.astype(jnp.bfloat16), preferred_element_type=jnp.float32)
+            out = jnp.where(visible > 0, out * (1.0 / jnp.where(visible > 0, total, 1.0)), 0.0)
+            at = (j * group + g) * HD
+            cross_ref[:, at:at + HD] = out.astype(jnp.bfloat16).T
 
     def attend(items):
-        js = [j for j, _, _ in items]
-        olds, totals, accs = [run_max[j] for j in js], [run_sum[j] for j in js], [run_out[j] for j in js]
-        scs = [scores(j, key_rows) for j, key_rows, _ in items]
-        tops = [jnp.maximum(old, jnp.max(sc, axis=0, keepdims=True)) for old, sc in zip(olds, scs)]
-        ws = [jnp.exp2(sc - top) for sc, top in zip(scs, tops)]
-        factors = [jnp.exp2(old - top) for old, top in zip(olds, tops)]
-        totals = [
-            total * factor + jnp.sum(w, axis=0, keepdims=True)
-            for total, factor, w in zip(totals, factors, ws)
-        ]
-        accs = [
-            acc * factor + jnp.dot(cols, w.astype(jnp.bfloat16), preferred_element_type=jnp.float32)
-            for acc, factor, (_, _, cols), w in zip(accs, factors, items, ws)
-        ]
-        for j, top, total, acc in zip(js, tops, totals, accs):
-            run_max[j], run_sum[j], run_out[j] = top, total, acc
+        for cols in tiles:
+            js = [j for j, _, _ in items]
+            olds = [run_max[j, :, cols] for j in js]
+            totals = [run_sum[j, :, cols] for j in js]
+            accs = [run_out[j, :, cols] for j in js]
+            scs = [scores(j, key_rows, cols) for j, key_rows, _ in items]
+            tops = [jnp.maximum(old, jnp.max(sc, axis=0, keepdims=True)) for old, sc in zip(olds, scs)]
+            ws = [jnp.exp2(sc - top) for sc, top in zip(scs, tops)]
+            factors = [jnp.exp2(old - top) for old, top in zip(olds, tops)]
+            totals = [
+                total * factor + jnp.sum(w, axis=0, keepdims=True)
+                for total, factor, w in zip(totals, factors, ws)
+            ]
+            accs = [
+                acc * factor + jnp.dot(vt, w.astype(jnp.bfloat16), preferred_element_type=jnp.float32)
+                for acc, factor, (_, _, vt), w in zip(accs, factors, items, ws)
+            ]
+            for j, top, total, acc in zip(js, tops, totals, accs):
+                run_max[j, :, cols], run_sum[j, :, cols], run_out[j, :, cols] = top, total, acc
 
     def attend_part(b, j, ss):
         cols = jnp.concatenate([kv[b, j, ss, 1, i:i + HD] for i in range(0, part, HD)], axis=1)

time: 27 us -> 27.4 us (1.015)
  Pallas kernels: 24.6 us -> 25 us
    pallas_call x1, Pallas kernels: 24.6 us -> 25 us  [local(): pl.pallas_call(functools.partial(kernel, n, subs), out_shape=(out, out),...]
where the time goes in v6:
time: 27.4 us; the launch traced here: 27.2 us
  Pallas kernels  25 us (91%)
  local copies, waits for them, and re-layouts  1.59 us (6%)
  between operations  0.64 us (2%)
    pallas_call x1, Pallas kernels, local(): pl.pallas_call(functools.partial(kernel, n, subs), out_shape=(out, out),...  25 us
    unnamed x2, local copies, waits for them, and re-layouts  1.59 us

profile of v6, /device:TPU:29, one launch (start us, length us, event | category | flops | bytes accessed | tf_op | source)
XLA Modules:
  0.0 27.2 jit_solution(9481628087015451027)
XLA Ops:
  0.6 25.0 %shard_map.86 = (bf16[128,2048]{1,0:T(8,128)(2,1)S(1)}, bf16[128,2048]{1,0:T(8,128)(2,1)S(1)}) custom-call(s32[8]{0:T(128)} %len_hbm.1, s32[8,128]{1,0:T(8,128)} %bitcast.1, bf16[128,2048]{1,0:T(8,128)(2,1)} %q_hbm.1, bf16[256,512]{1,0:T(8,128)(2,1)} %k_hbm.1, bf16[256,512]{1,0:T(8,128)(2,1)} %v_hbm.1, bf16[16,512]{1,0:T(8,128)(2,1)} %ik_hbm.1, ...), custom_call_target="tpu_custom_call" | custom-call | tf_op jit(solution)/shard_map/pallas_call | solution.py:315
  25.6 0.8 %copy.11 = bf16[128,2048]{1,0:T(8,128)(2,1)} copy(bf16[128,2048]{1,0:T(8,128)(2,1)S(1)} %get-tuple-element.2) | data formatting | bytes 1048576
  26.4 0.8 %copy.12 = bf16[128,2048]{1,0:T(8,128)(2,1)} copy(bf16[128,2048]{1,0:T(8,128)(2,1)S(1)} %get-tuple-element.3) | data formatting | bytes 1048576

commit v7 on v5

--- a/solution.py
+++ b/solution.py
@@ -61,8 +61,6 @@
     loads[0].wait()
     loads[1].wait()
     lay_out(s)
-    loads[2].wait()
-    loads[3].wait()
     pl.semaphore_wait(barrier, n - 1 + subs - 1)
 
     def up(b, j):
@@ -90,17 +88,20 @@
             device_id=sibling(d), device_id_type=MESH,
         )
 
+    @pl.when(c < n - 1)
+    def _():
+        for j in range(heads):
+            up(c, j).start()
+
+    loads[2].wait()
+    loads[3].wait()
+
     @pl.loop(1, n)
     def _(d):
         image_to(d).start()
 
     for d in range(1, subs):
         image_side(c, s, d).start()
-
-    @pl.when(c < n - 1)
-    def _():
-        for j in range(heads):
-            up(c, j).start()
 
     for d in range(1, subs):
         lay_out(lax.rem(s + d, subs))

time: 27 us -> 30.5 us (1.13)
  Pallas kernels: 24.6 us -> 28.1 us
    pallas_call x1, Pallas kernels: 24.6 us -> 28.1 us  [local(): pl.pallas_call(functools.partial(kernel, n, subs), out_shape=(out, out),...]
where the time goes in v7:
time: 30.5 us; the launch traced here: 30.3 us
  Pallas kernels  28.1 us (92%)
  local copies, waits for them, and re-layouts  1.59 us (5%)
  between operations  0.64 us (2%)
    pallas_call x1, Pallas kernels, local(): pl.pallas_call(functools.partial(kernel, n, subs), out_shape=(out, out),...  28.1 us
    unnamed x2, local copies, waits for them, and re-layouts  1.59 us

profile of v7, /device:TPU:29, one launch (start us, length us, event | category | flops | bytes accessed | tf_op | source)
XLA Modules:
  0.0 30.3 jit_solution(10128552984606313166)
XLA Ops:
  0.6 28.1 %shard_map.86 = (bf16[128,2048]{1,0:T(8,128)(2,1)S(1)}, bf16[128,2048]{1,0:T(8,128)(2,1)S(1)}) custom-call(s32[8]{0:T(128)} %len_hbm.1, s32[8,128]{1,0:T(8,128)} %bitcast.1, bf16[128,2048]{1,0:T(8,128)(2,1)} %q_hbm.1, bf16[256,512]{1,0:T(8,128)(2,1)} %k_hbm.1, bf16[256,512]{1,0:T(8,128)(2,1)} %v_hbm.1, bf16[16,512]{1,0:T(8,128)(2,1)} %ik_hbm.1, ...), custom_call_target="tpu_custom_call" | custom-call | tf_op jit(solution)/shard_map/pallas_call | solution.py:313
  28.8 0.8 %copy.11 = bf16[128,2048]{1,0:T(8,128)(2,1)} copy(bf16[128,2048]{1,0:T(8,128)(2,1)S(1)} %get-tuple-element.2) | data formatting | bytes 1048576
  29.5 0.8 %copy.12 = bf16[128,2048]{1,0:T(8,128)(2,1)} copy(bf16[128,2048]{1,0:T(8,128)(2,1)S(1)} %get-tuple-element.3) | data formatting | bytes 1048576
